TPU v7x, 512 devices: a whole 4x8x8 slice. The times are simulated.
512 devices in a mesh: row: 32 (over y, x_hi, core), col: 16 (over z, x_lo).
Axes of the slice: x: 4 (x_hi: 2, x_lo: 2; x = x_hi * 2 + x_lo), y: 8, z: 8, core: 2. Of those that a mesh axis runs over, the one named last changes fastest.
Arguments:
- pair: float32 [256, 256, 128], P('row', 'col'), may hold values from -6 to 6
- pair_mask: int32 [256, 256], P('row', 'col'), may hold values 0 or 1
- w_project: bfloat16 [2, 128, 512], replicated, may hold values from -0.5 to 0.5
- w_gate: bfloat16 [2, 128, 128], replicated, may hold values from -0.5 to 0.5
- w_output: bfloat16 [2, 128, 128], replicated, may hold values from -0.5 to 0.5
Outputs:
- updated: float32 [256, 256, 128], P('row', 'col')
All inputs are finite; a program needn't handle non-finite values. No bound on the sum of `pair_mask` on one device may be relied on, other than what follows from the above.
Results may differ from a plain program's by a relative error of at most 0.0046.
Values may be sent and summed in bfloat16 or wider, within the bound.
A program may use at most 64 MiB of HBM per device.

v0:
```python
import jax
import jax.numpy as jnp
from jax import lax
from jax.sharding import PartitionSpec as P

H = 128


def spread_2(value, axis, source):
    kept = jnp.where(lax.axis_index(axis) == source, value, 0).astype(value.dtype)
    return lax.psum(kept, axis)


def norm_last(values):
    center = values - jnp.mean(values, axis=-1, keepdims=True)
    spread = jnp.mean(center * center, axis=-1, keepdims=True)
    return center * lax.rsqrt(spread + 1e-05)


def operands(state, mask_f, w_proj, w_gt):
    normed = norm_last(state).astype(jnp.bfloat16)
    proj = jnp.einsum("ijc,cd->ijd", normed, w_proj, preferred_element_type=jnp.float32)
    weight = mask_f[..., None]
    left = (weight * jax.nn.sigmoid(proj[..., :H]) * proj[..., H : 2 * H]).astype(jnp.bfloat16)
    right = (weight * jax.nn.sigmoid(proj[..., 2 * H : 3 * H]) * proj[..., 3 * H :]).astype(
        jnp.bfloat16
    )
    gate = jax.nn.sigmoid(
        jnp.einsum("ijc,cd->ijd", normed, w_gt, preferred_element_type=jnp.float32)
    )
    return (left, right, gate)


def finish(state, tri, gate, w_out):
    tnorm = norm_last(tri).astype(jnp.bfloat16)
    result = jnp.einsum("ijh,hc->ijc", tnorm, w_out, preferred_element_type=jnp.float32)
    return state + gate * result


def per_device(pair, pair_mask, w_project, w_gate, w_output):
    mask_f = pair_mask.astype(jnp.float32)
    ratio = lax.axis_size("row") // lax.axis_size("col")
    block_rows = pair.shape[0]
    col_index = lax.axis_index("col")
    row_index = lax.axis_index("row")
    left, right, gate = operands(pair, mask_f, w_project[0], w_gate[0])
    left_rows, right_full = (
        lax.all_gather(left, "col", axis=1, tiled=True),
        lax.all_gather(right, "col", axis=1, tiled=True),
    )
    pieces = []
    for step in range(ratio):
        pieces.append(spread_2(right_full, "row", col_index * ratio + step))
    right_cols = jnp.concatenate(pieces, axis=0)
    tri = jnp.einsum("ikh,jkh->ijh", left_rows, right_cols, preferred_element_type=jnp.float32)
    state = finish(pair, tri, gate, w_output[0])
    left, right, gate = operands(state, mask_f, w_project[1], w_gate[1])
    left_all, right_all = (
        lax.all_gather(left, "row", axis=0, tiled=True),
        lax.all_gather(right, "row", axis=0, tiled=True),
    )
    offset = row_index % ratio * block_rows
    picked = lax.dynamic_slice_in_dim(left_all, offset, block_rows, 1)
    left_need = spread_2(picked, "col", row_index // ratio)
    tri = jnp.einsum("kih,kjh->ijh", left_need, right_all, preferred_element_type=jnp.float32)
    return finish(state, tri, gate, w_output[1])


def solution(mesh):
    in_specs = (P("row", "col", None), P("row", "col"), P(), P(), P())
    out_specs = P("row", "col", None)
    return jax.shard_map(
        per_device, mesh=mesh, in_specs=in_specs, out_specs=out_specs, check_vma=False
    )
```

profile of v0, /device:TPU:1, one launch (start us, length us, event | category | flops | bytes accessed | tf_op | source)
XLA Modules:
  0.0 644.1 jit_solution(1692496053743199080)
XLA Ops:
  6.5 1.0 reduce_sum.72
  7.6 1.0 multiply_reduce_fusion.3
  8.6 0.7 convert_element_type.33
  9.3 1.2 fusion.10
  10.5 36.6 %all_gather.12 = bf16[8,256,128]{2,1,0:T(8,128)(2,1)S(1)} all-gather(bf16[8,16,128]{2,1,0:T(8,128)(2,1)S(1)} %get-tuple-element.12), channel_id=1, replica_groups=mesh['row'=32,'col'=16] {'col'}, dimensions={1}, use_global_device_ids=true | all-gather | bytes 557056 | tf_op jit(solution)/shard_map/all_gather | solution.py:49
  47.1 1.1 broadcast_select_fusion.2
  48.3 26.0 %all_gather.13 = bf16[8,256,128]{2,1,0:T(8,128)(2,1)S(1)} all-gather(bf16[8,16,128]{2,1,0:T(8,128)(2,1)S(1)} %get-tuple-element.11), channel_id=1, replica_groups=mesh['row'=32,'col'=16] {'col'}, dimensions={1}, use_global_device_ids=true | all-gather | bytes 557056 | tf_op jit(solution)/shard_map/all_gather | solution.py:48
  74.3 0.4 copy.19
  74.7 1.1 fusion.7
  75.8 251.7 %all-reduce.6.cloned.1.call-done = (bf16[8,256,128]{2,1,0:T(8,128)(2,1)}, bf16[8,256,128]{2,1,0:T(8,128)(2,1)}) async-done(((bf16[8,256,128]{2,1,0:T(8,128)(2,1)}, bf16[8,256,128]{2,1,0:T(8,128)(2,1)}), (bf16[8,256,128]{2,1,0:T(8,128)(2,1)}, bf16[8,256,128]{2,1,0:T(8,128)(2,1)})) %all-reduce.6.cloned.1.call-update) | async-done | bytes 1048592 | tf_op jit(solution)/shard_map/psum | solution.py:11
  327.5 1.3 pad_maximum_fusion
  328.8 0.9 copy.18
  329.7 0.4 fusion.47
  331.4 0.7 fusion.14
  332.2 0.7 all-gather.3.cloned.1.call-update
  332.9 81.9 %all-gather.5.cloned.1.call-done = bf16[256,16,128]{2,1,0:T(8,128)(2,1)} async-done(((bf16[8,16,128]{2,1,0:T(8,128)(2,1)}), bf16[256,16,128]{2,1,0:T(8,128)(2,1)}) %all-gather.5.cloned.1.call-update) | async-done | bytes 1048592 | tf_op jit(solution)/shard_map/all_gather | solution.py:59
  414.9 1.1 constant_dynamic-slice_fusion
  415.9 0.6 copy.24
  416.5 0.8 broadcast_select_fusion
  417.6 81.1 %all-gather.3.cloned.1.call-done = bf16[256,16,128]{2,1,0:T(8,128)(2,1)} async-done(((bf16[8,16,128]{2,1,0:T(8,128)(2,1)}), bf16[256,16,128]{2,1,0:T(8,128)(2,1)}) %all-gather.3.cloned.1.call-update) | async-done | bytes 1048592 | tf_op jit(solution)/shard_map/all_gather | solution.py:60
  498.7 7.5 %copy.22 = bf16[256,16,128]{1,0,2:T(8,128)(2,1)} copy(bf16[256,16,128]{2,1,0:T(8,128)(2,1)} %all-gather.3.cloned.1.call-done) | data formatting | bytes 2097152 | tf_op jit(solution)/shard_map/all_gather | solution.py:60
  506.3 125.4 %all-reduce.4.cloned.1.call-done = bf16[256,8,128]{0,1,2:T(8,128)(2,1)} async-done(((bf16[256,8,128]{0,1,2:T(8,128)(2,1)}), bf16[256,8,128]{0,1,2:T(8,128)(2,1)}) %all-reduce.4.cloned.1.call-update) | async-done | bytes 524304 | tf_op jit(solution)/shard_map/psum | solution.py:11
  631.6 4.6 fusion.48
  636.7 0.9 fusion
  (34 shorter events, 2.2 us)
Async XLA Ops:
  6.5 324.1 %copy-start = (f32[8,16,128]{2,1,0:T(8,128)S(1)}, f32[8,16,128]{2,1,0:T(8,128)}, u32[]{:S(2)}) copy-start(f32[8,16,128]{2,1,0:T(8,128)} %param.5) | copy-start | bytes 196612
  6.5 324.6 %copy-start.1 = (bf16[2,128,512]{2,1,0:T(8,128)(2,1)S(1)}, bf16[2,128,512]{2,1,0:T(8,128)(2,1)}, u32[]{:S(2)}) copy-start(bf16[2,128,512]{2,1,0:T(8,128)(2,1)} %param.7) | copy-start | bytes 786436
  6.5 324.1 %copy-start.2 = (bf16[2,128,128]{2,1,0:T(8,128)(2,1)S(1)}, bf16[2,128,128]{2,1,0:T(8,128)(2,1)}, u32[]{:S(2)}) copy-start(bf16[2,128,128]{2,1,0:T(8,128)(2,1)} %param.9) | copy-start | bytes 196612
  6.5 321.0 %all-reduce.6.cloned.1.call-start = ((), (), s32[]{:S(2)}) async-start(), calls=%async_computation.3 | async-start | bytes 2097152 | tf_op jit(solution)/shard_map/psum | solution.py:11
  47.1 370.3 %copy-start.3 = (bf16[2,128,128]{2,1,0:T(8,128)(2,1)S(1)}, bf16[2,128,128]{2,1,0:T(8,128)(2,1)}, u32[]{:S(2)}) copy-start(bf16[2,128,128]{2,1,0:T(8,128)(2,1)} %param.8) | copy-start | bytes 196612
  48.2 366.6 %all-gather.5.cloned.1.call-start = ((), (), s32[]{:S(2)}) async-start(), calls=%async_computation.1 | async-start | bytes 1081344 | tf_op jit(solution)/shard_map/all_gather | solution.py:59
  332.1 166.6 %all-gather.3.cloned.1.call-start = ((), (), s32[]{:S(2)}) async-start(), calls=%async_computation | async-start | bytes 1081344 | tf_op jit(solution)/shard_map/all_gather | solution.py:60
  332.9 298.8 %all-reduce.4.cloned.1.call-start = ((), (), s32[]{:S(2)}) async-start(), calls=%async_computation.2 | async-start | bytes 1048576 | tf_op jit(solution)/shard_map/psum | solution.py:11
Sparse Core Ops, SparseCore 0:
  48.4 279.1 all-reduce.5
  332.2 82.5 all-gather.4
  418.8 79.9 all-gather.2
  501.7 129.8 all-reduce.3
where the time goes:
time: 654 us; the launch traced here: 644 us
  waiting for transfers between devices  541 us (83%)
  blocking collectives  62.6 us (10%)
  between operations  13.4 us (2%)
  local copies, waits for them, and re-layouts  10.9 us (2%)
  matrix products  8.81 us (1%)
  other arithmetic  7.45 us (1%)
    psum x2, waiting for transfers between devices, spread_2(): return lax.psum(kept, axis)  377 us
    all_gather x1, waiting for transfers between devices, per_device(): lax.all_gather(left, 'row', axis=0, tiled=True)  81.9 us
    all_gather x1, waiting for transfers between devices, per_device(): lax.all_gather(right, 'row', axis=0, tiled=True)  81.1 us
    all_gather x1, blocking collectives, per_device(): lax.all_gather(right, 'col', axis=1, tiled=True)  36.6 us
    all_gather x1, blocking collectives, per_device(): lax.all_gather(left, 'col', axis=1, tiled=True)  26 us
  transfers between devices with their start and end apart: 4, of which 4 were waited for; matrix products, arithmetic and copies ran while one was open for 2% of the time, Pallas kernels for 0%

commit v1 on v0

v1 whole, which is shorter than its diff:
```python
import functools

import jax
import jax.numpy as jnp
from jax import lax
from jax.experimental import pallas as pl
from jax.experimental.pallas import tpu as pltpu
from jax.sharding import PartitionSpec as P

MESH = pl.DeviceIdType.MESH
F32, BF16 = jnp.float32, jnp.bfloat16
GROUP, RING, BLOCK, SHARE = 8, 8, 32, 16
HALF = RING // 2


def coordinates():
    row, col = lax.axis_index("row"), lax.axis_index("col")
    x_hi, x_lo, core = (row // 2) % 2, col % 2, row % 2
    return (x_hi * 2 + x_lo) * 2 + core, row // 4, col // 2


def device(g, y, z):
    return ((y * 2 + g // 4) * 2 + g % 2, z * 2 + (g // 2) % 2)


def ahead(index, by):
    return lax.rem(index + by, 8)


def barrel(parts):
    block = lax.broadcasted_iota(jnp.int32, parts[0].shape, 1) // SHARE
    for bit in (1, 2, 4):
        odd = (block // bit) % 2 == 1
        parts = [jnp.where(odd, parts[(m + bit) % 8], parts[m]) for m in range(8)]
    return parts


def rolled(parts):
    return [parts[0]] + [pltpu.roll(parts[m], SHARE * m, 1) for m in range(1, 8)]


def swap_blocks(parts):
    out = barrel(rolled(barrel(parts)))
    return [out[-g % 8] for g in range(8)]


def fold_blocks(parts):
    turned = rolled(barrel(parts))
    while len(turned) > 1:
        turned = [a + b for a, b in zip(turned[::2], turned[1::2])]
    return turned[0]


def norm_last(values):
    center = values - jnp.mean(values, axis=-1, keepdims=True)
    spread = jnp.mean(center * center, axis=-1, keepdims=True)
    return center * lax.rsqrt(spread + 1e-05)


def operands(normed, weight, w_proj):
    proj = jnp.dot(normed, w_proj, preferred_element_type=F32)
    left = weight * jax.nn.sigmoid(proj[:, :128]) * proj[:, 128:256]
    right = weight * jax.nn.sigmoid(proj[:, 256:384]) * proj[:, 384:]
    return left, right


def kernel(pair, mask, w_project, w_gate, w_output, out, x, wp, wg, wo, mask_rows, gate, send_l, send_r, a_buf, b_buf, a_f, b_f, acc, t_send, t_buf, in_sem, s_sem, r_sem):
    g, y, z = coordinates()
    bar = pltpu.get_barrier_semaphore()
    turned = [(ahead(z, HALF), y), (z, ahead(y, HALF))]

    def signal(*who):
        pl.semaphore_signal(bar, inc=1, device_id=device(*who), device_id_type=MESH)

    loads = [
        pltpu.make_async_copy(source, target, in_sem.at[i])
        for i, (source, target) in enumerate([(pair, x), (w_project, wp), (w_gate, wg), (w_output, wo)])
    ]
    for load in loads:
        load.start()
    for d in range(8):
        for ty, tz in turned:
            signal(ahead(g, d), ty, tz)
    for d in range(1, 8):
        signal(g, y, ahead(z, d))
        signal(g, ahead(y, d), z)
        signal(ahead(g, d), y, z)

    def remote(u, n, source, target, who):
        return pltpu.make_async_remote_copy(
            src_ref=source, dst_ref=target, send_sem=s_sem.at[u, n], recv_sem=r_sem.at[u, n],
            device_id=device(*who), device_id_type=MESH,
        )

    def share_copy(u, d, sending):
        send, buf = (send_l, a_buf) if u == 0 else (send_r, b_buf)
        to = ahead(g, d)
        slot = g if sending else ahead(g, 8 - d)
        return remote(u, d - 1, send.at[u, to], buf.at[u, 0, slot], (to, y, z))

    def turn_copy(u, d, sending):
        send, buf = (send_r, b_buf) if u == 0 else (send_l, a_buf)
        to = ahead(g, d)
        slot = g if sending else ahead(g, 8 - d)
        return remote(u, 7 + d, send.at[u, to], buf.at[u, 0, slot], (to, *turned[u]))

    def z_copy(u, d, sending):
        return remote(u, 14 + d, a_buf.at[u, 0], a_buf.at[u, 8 - d], (g, y, ahead(z, d)))

    def y_copy(u, d, sending):
        return remote(u, 21 + d, b_buf.at[u, 0], b_buf.at[u, 8 - d], (g, ahead(y, d), z))

    def back_copy(u, d, sending):
        to = ahead(g, d)
        slot = g if sending else ahead(g, 8 - d)
        return remote(u, 28 + d, t_send.at[u, to], t_buf.at[u, slot], (to, y, z))

    FAR_FIRST = (4, 3, 5, 2, 6, 1, 7)

    def pack(u, left, right):
        both = jnp.concatenate([left.reshape(8, 16, 128), right.reshape(8, 16, 128)], axis=1)
        pieces = swap_blocks([both[k] for k in range(8)])
        for p in range(8):
            send_l[u, p] = pieces[p][:16].astype(BF16)
            send_r[u, p] = pieces[p][16:].astype(BF16)

    def exchange(u):
        for d in range(8):
            turn_copy(u, d, True).start()
        for d in range(1, 8):
            share_copy(u, d, True).start()
        stay, stay_buf = (send_l, a_buf) if u == 0 else (send_r, b_buf)
        stay_buf[u, 0, g] = stay[u, g]
        normed = norm_last(x[...]).astype(BF16)
        gate[...] = jax.nn.sigmoid(jnp.dot(normed, wg[u], preferred_element_type=F32))
        acc[...] = jnp.zeros_like(acc)
        stay_copy, cross_copy = (z_copy, y_copy) if u == 0 else (y_copy, z_copy)
        for d in range(1, 8):
            share_copy(u, d, False).wait_recv()
        for d in FAR_FIRST:
            stay_copy(u, d, True).start()
        for d in range(8):
            turn_copy(u, d, False).wait_recv()
        for d in FAR_FIRST:
            cross_copy(u, d, True).start()
        for d in range(1, 8):
            stay_copy(u, d, False).wait_recv()

    def widen(u, source, target):
        for p in range(8):
            x_hi, x_lo, core = p // 4, (p // 2) % 2, p % 2
            piece = source[p].astype(F32)
            if u == 0:
                first = (x_hi * 2 + core) * 8
                target[x_lo * 2, first : first + 8] = piece[:8]
                target[x_lo * 2 + 1, first : first + 8] = piece[8:]
            else:
                target[x_hi * 2 + core, x_lo * 16 : x_lo * 16 + 16] = piece

    def multiply(u):
        cross_sem0 = 21 if u == 0 else 14

        def block(t, _):
            odd = lax.rem(t, 2)
            cross = odd * ((t + 1) // 2) + (1 - odd) * lax.rem(8 - t // 2, 8)
            stay = lax.rem(cross + HALF + 8 + (y - z if u == 0 else z - y), 8)
            cross_buf = b_buf if u == 0 else a_buf

            @pl.when(t > 0)
            def _():
                n = cross_sem0 + 8 - cross
                remote(u, n, cross_buf.at[u, 0], cross_buf.at[u, cross], (g, y, z)).wait_recv()

            a_slot, b_slot = (stay, cross) if u == 0 else (cross, stay)
            widen(u, a_buf.at[u, a_slot], a_f)
            widen(u, b_buf.at[u, b_slot], b_f)

            def rows(c, _):
                total = [acc[c * 8 + i] for i in range(8)]
                for k in range(4):
                    b = b_f[k]
                    for i in range(8):
                        total[i] = total[i] + a_f[k, pl.ds(c * 8 + i, 1), :] * b
                for i in range(8):
                    acc[c * 8 + i] = total[i]
                return 0

            lax.fori_loop(0, 4, rows, 0)
            return 0

        lax.fori_loop(0, 8, block, 0)

    def give_back(u):
        def piece(d, _):
            to = ahead(g, 8 - d)
            row0, col0 = (to // 4 * 2 + to % 2) * 8, pl.multiple_of((to // 2) % 2 * 16, 16)
            t_send[u, to] = fold_blocks([acc[row0 + i, pl.ds(col0, 16), :] for i in range(8)])

            @pl.when(d < 8)
            def _():
                n = 28 + 8 - d
                remote(u, n, t_send.at[u, to], t_buf.at[u, g], (to, y, z)).start()

            return 0

        lax.fori_loop(1, 9, piece, 0)
        t_buf[u, g] = t_send[u, g]

    def finish(u):
        for d in range(1, 8):
            back_copy(u, d, False).wait_recv()
        tri = jnp.concatenate(swap_blocks([t_buf[u, p] for p in range(8)]), axis=0)
        tnorm = norm_last(tri).astype(BF16)
        result = jnp.dot(tnorm, wo[u], preferred_element_type=F32)
        return x[...] + gate[...] * result

    loads[0].wait()
    mask_f = mask[...].astype(F32)
    r = lax.broadcasted_iota(jnp.int32, (128, 128), 0)
    c = lax.broadcasted_iota(jnp.int32, (128, 128), 1)
    spread = jnp.concatenate([jnp.broadcast_to(mask_f[i : i + 1, :], (16, 16)) for i in range(8)], axis=0)
    picked = jnp.where(r[:, :16] % 16 == c[:, :16], spread, 0.0)
    mask_rows[...] = jnp.broadcast_to(jnp.sum(picked, axis=1, keepdims=True), (128, 128))

    columns = [x[pl.ds(k, 8, stride=16), :] for k in range(16)]
    weight = jnp.concatenate([jnp.broadcast_to(mask_f[:, k : k + 1], (8, 128)) for k in range(16)], axis=0)
    normed = norm_last(jnp.concatenate(columns, axis=0)).astype(BF16)
    loads[1].wait()
    left, right = operands(normed, weight, wp[0])
    order = lambda v: jnp.swapaxes(v.reshape(2, 8, 8, 128), 0, 1)
    pack(0, order(left), order(right))
    loads[2].wait()
    loads[3].wait()
    pl.semaphore_wait(bar, 16 + 21)
    exchange(0)
    multiply(0)
    give_back(0)
    x[...] = finish(0)

    normed = norm_last(x[...]).astype(BF16)
    left, right = operands(normed, mask_rows[...], wp[1])
    pack(1, left, right)
    exchange(1)
    multiply(1)
    give_back(1)
    out[...] = finish(1)

    for u in range(2):
        for d in range(8):
            turn_copy(u, d, True).wait_send()
        for d in range(1, 8):
            for copy in (share_copy, z_copy, y_copy, back_copy):
                copy(u, d, True).wait_send()


def per_device(pair, pair_mask, w_project, w_gate, w_output):
    any_space = pl.BlockSpec(memory_space=pl.ANY)
    vmem = pl.BlockSpec(memory_space=pltpu.VMEM)
    updated = pl.pallas_call(
        kernel,
        name="triangle",
        out_shape=jax.ShapeDtypeStruct((128, 128), F32),
        in_specs=[any_space, vmem, any_space, any_space, any_space],
        out_specs=vmem,
        scratch_shapes=[
            pltpu.VMEM((128, 128), F32),
            pltpu.VMEM((2, 128, 512), BF16),
            pltpu.VMEM((2, 128, 128), BF16),
            pltpu.VMEM((2, 128, 128), BF16),
            pltpu.VMEM((128, 128), F32),
            pltpu.VMEM((128, 128), F32),
            pltpu.VMEM((2, 8, 16, 128), BF16),
            pltpu.VMEM((2, 8, 16, 128), BF16),
            pltpu.VMEM((2, 8, 8, 16, 128), BF16),
            pltpu.VMEM((2, 8, 8, 16, 128), BF16),
            pltpu.VMEM((4, 32, 128), F32),
            pltpu.VMEM((4, 32, 128), F32),
            pltpu.VMEM((32, 32, 128), F32),
            pltpu.VMEM((2, 8, 16, 128), F32),
            pltpu.VMEM((2, 8, 16, 128), F32),
            pltpu.SemaphoreType.DMA((4,)),
            pltpu.SemaphoreType.DMA((2, 36)),
            pltpu.SemaphoreType.DMA((2, 36)),
        ],
        compiler_params=pltpu.CompilerParams(
            collective_id=0, has_side_effects=True, vmem_limit_bytes=32 * 1024 * 1024
        ),
    )(pair.reshape(128, 128), pair_mask, w_project, w_gate, w_output)
    return updated.reshape(pair.shape)


def solution(mesh):
    in_specs = (P("row", "col", None), P("row", "col"), P(), P(), P())
    return jax.shard_map(
        per_device, mesh=mesh, in_specs=in_specs, out_specs=P("row", "col", None), check_vma=False
    )
```

time: 654 us -> 62.8 us (0.10); the launches traced: 644 us -> 62.5 us
  waiting for transfers between devices: 541 us -> 0 us
  blocking collectives: 62.6 us -> 0 us
  Pallas kernels: 0 us -> 57.7 us
  between operations: 13.4 us -> 0.01 us
  matrix products: 8.81 us -> 0 us
  other arithmetic: 7.45 us -> 0 us
    psum x2 -> x0, waiting for transfers between devices: 377 us -> none  [spread_2(): return lax.psum(kept, axis)]
    all_gather x2 -> x0, waiting for transfers between devices: 163 us -> none  [the longest x1 81.9 us: per_device(): lax.all_gather(left, 'row', axis=0, tiled=True)]
    all_gather x2 -> x0, blocking collectives: 62.6 us -> none  [the longest x1 36.6 us: per_device(): lax.all_gather(right, 'col', axis=1, tiled=True)]
    pallas_call x0 -> x1, Pallas kernels: none -> 57.7 us  [per_device(): pl.pallas_call(kernel, name='triangle', out_shape=jax.ShapeDtypeStruct((1...]
    dot_general x8 -> x0, matrix products: 8.81 us -> none  [the longest x1 4.61 us: per_device(): jnp.einsum('kih,kjh->ijh', left_need, right_all, preferred_element_type=j...]
    all_gather x2 -> x0, local copies, waits for them, and re-layouts: 7.94 us -> none  [the longest x1 7.55 us: per_device(): lax.all_gather(right, 'row', axis=0, tiled=True)]
  transfers between devices with their start and end apart: 4 -> 0, of which waited for: 4 -> 0; matrix products, arithmetic and copies ran while one was open for 2% -> 0% of each run, Pallas kernels for 0% -> 0%
where the time goes in v1:
time: 62.8 us; the launch traced here: 62.5 us
  Pallas kernels  57.7 us (92%)
  local copies, waits for them, and re-layouts  4.78 us (8%)
    pallas_call x1, Pallas kernels, per_device(): pl.pallas_call(kernel, name='triangle', out_shape=jax.ShapeDtypeStruct((1...  57.7 us
    unnamed x11, local copies, waits for them, and re-layouts  4.78 us

profile of v1, /device:TPU:1, one launch (start us, length us, event | category | flops | bytes accessed | tf_op | source)
XLA Modules:
  0.0 62.5 jit_solution(16925921250241958546)
XLA Ops:
  0.0 0.0 copy-start
  0.0 0.9 %copy-done = bf16[2,128,512]{2,1,0:T(8,128)(2,1)S(1)} copy-done((bf16[2,128,512]{2,1,0:T(8,128)(2,1)S(1)}, bf16[2,128,512]{2,1,0:T(8,128)(2,1)}, u32[]{:S(2)}) %copy-start) | copy-done | bytes 262168
  1.0 0.0 copy-start.1
  1.0 0.8 %copy-done.1 = f32[8,16,128]{2,1,0:T(8,128)S(1)} copy-done((f32[8,16,128]{2,1,0:T(8,128)S(1)}, f32[8,16,128]{2,1,0:T(8,128)}, u32[]{:S(2)}) %copy-start.1) | copy-done | bytes 65560
  1.8 0.0 copy-start.2
  1.8 0.8 %copy-done.2 = bf16[2,128,128]{2,1,0:T(8,128)(2,1)S(1)} copy-done((bf16[2,128,128]{2,1,0:T(8,128)(2,1)S(1)}, bf16[2,128,128]{2,1,0:T(8,128)(2,1)}, u32[]{:S(2)}) %copy-start.2) | copy-done | bytes 65560
  2.6 0.0 copy-start.3
  2.6 0.8 %copy-done.3 = bf16[2,128,128]{2,1,0:T(8,128)(2,1)S(1)} copy-done((bf16[2,128,128]{2,1,0:T(8,128)(2,1)S(1)}, bf16[2,128,128]{2,1,0:T(8,128)(2,1)}, u32[]{:S(2)}) %copy-start.3) | copy-done | bytes 65560
  3.5 0.0 copy-start.4
  3.5 0.7 %copy-done.4 = s32[8,16]{1,0:T(8,128)S(1)} copy-done((s32[8,16]{1,0:T(8,128)S(1)}, s32[8,16]{1,0:T(8,128)}, u32[]{:S(2)}) %copy-start.4) | copy-done | bytes 536
  4.2 57.7 %triangle.1 = f32[128,128]{1,0:T(8,128)S(1)} custom-call(f32[128,128]{1,0:T(8,128)S(1)} %bitcast.3, s32[8,16]{1,0:T(8,128)S(1)} %copy-done.4, bf16[2,128,512]{2,1,0:T(8,128)(2,1)S(1)} %copy-done, bf16[2,128,128]{2,1,0:T(8,128)(2,1)S(1)} %copy-done.2, bf16[2,128,128]{2,1,0:T(8,128)(2,1)S(1)} %copy-done.3), custom_call_target="tpu_custom_call" | custom-call | tf_op jit(solution)/shard_map/triangle/pallas_call | solution.py:259
  61.9 0.6 %copy.7 = f32[8,16,128]{2,1,0:T(8,128)} copy(f32[8,16,128]{2,1,0:T(8,128)S(1)} %bitcast.2) | data formatting | bytes 131072
Async XLA Ops:
  0.0 0.9 %copy-start = (bf16[2,128,512]{2,1,0:T(8,128)(2,1)S(1)}, bf16[2,128,512]{2,1,0:T(8,128)(2,1)}, u32[]{:S(2)}) copy-start(bf16[2,128,512]{2,1,0:T(8,128)(2,1)} %w_project.1) | copy-start | bytes 786436
  1.0 0.8 %copy-start.1 = (f32[8,16,128]{2,1,0:T(8,128)S(1)}, f32[8,16,128]{2,1,0:T(8,128)}, u32[]{:S(2)}) copy-start(f32[8,16,128]{2,1,0:T(8,128)} %param.5) | copy-start | bytes 196612
  1.8 0.8 %copy-start.2 = (bf16[2,128,128]{2,1,0:T(8,128)(2,1)S(1)}, bf16[2,128,128]{2,1,0:T(8,128)(2,1)}, u32[]{:S(2)}) copy-start(bf16[2,128,128]{2,1,0:T(8,128)(2,1)} %w_gate.1) | copy-start | bytes 196612
  2.6 0.8 %copy-start.3 = (bf16[2,128,128]{2,1,0:T(8,128)(2,1)S(1)}, bf16[2,128,128]{2,1,0:T(8,128)(2,1)}, u32[]{:S(2)}) copy-start(bf16[2,128,128]{2,1,0:T(8,128)(2,1)} %w_output.1) | copy-start | bytes 196612
  3.5 0.7 %copy-start.4 = (s32[8,16]{1,0:T(8,128)S(1)}, s32[8,16]{1,0:T(8,128)}, u32[]{:S(2)}) copy-start(s32[8,16]{1,0:T(8,128)} %mask.1) | copy-start | bytes 1540

commit v2 on v1

v2 whole, which is shorter than its diff:
```python
import jax
import jax.numpy as jnp
from jax import lax
from jax.experimental import pallas as pl
from jax.experimental.pallas import tpu as pltpu
from jax.sharding import PartitionSpec as P

MESH = pl.DeviceIdType.MESH
F32, BF16 = jnp.float32, jnp.bfloat16
GROUP, RING, BLOCK, SHARE = 8, 8, 32, 16
HALF = RING // 2


def coordinates():
    row, col = lax.axis_index("row"), lax.axis_index("col")
    x_hi, x_lo, core = (row // 2) % 2, col % 2, row % 2
    return (x_hi * 2 + x_lo) * 2 + core, row // 4, col // 2


def device(g, y, z):
    return ((y * 2 + g // 4) * 2 + g % 2, z * 2 + (g // 2) % 2)


def ahead(index, by):
    return lax.rem(index + by, 8)


def partner(g, e):
    x_hi, x_lo, core = g // 4, (g // 2) % 2, g % 2
    return ((x_hi + e // 4) % 2 * 2 + (x_lo + e // 2) % 2) * 2 + (core + e) % 2


def barrel(parts):
    block = lax.broadcasted_iota(jnp.int32, parts[0].shape, 1) // SHARE
    for bit in (1, 2, 4):
        odd = (block // bit) % 2 == 1
        parts = [jnp.where(odd, parts[(m + bit) % 8], parts[m]) for m in range(8)]
    return parts


def rolled(parts):
    return [parts[0]] + [pltpu.roll(parts[m], SHARE * m, 1) for m in range(1, 8)]


def swap_blocks(parts):
    out = barrel(rolled(barrel(parts)))
    return [out[-g % 8] for g in range(8)]


def fold_blocks(parts):
    turned = rolled(barrel(parts))
    while len(turned) > 1:
        turned = [a + b for a, b in zip(turned[::2], turned[1::2])]
    return turned[0]


def norm_last(values):
    center = values - jnp.mean(values, axis=-1, keepdims=True)
    spread = jnp.mean(center * center, axis=-1, keepdims=True)
    return center * lax.rsqrt(spread + 1e-05)


def kernel(pair, mask, w_project, w_gate, w_output, out, x, mk, wp, wg, wo, mask_rows, gate, send_l, send_r, a_buf, b_buf, a_f, b_f, acc, t_send, t_buf, in_sem, s_sem, r_sem):
    g, y, z = coordinates()
    bar = pltpu.get_barrier_semaphore()
    turned = [(ahead(2 * y + HALF + 8, 8 - z), y), (z, ahead(2 * z + HALF + 8, 8 - y))]

    def signal(*who):
        pl.semaphore_signal(bar, inc=1, device_id=device(*who), device_id_type=MESH)

    loads = [
        pltpu.make_async_copy(source, target, in_sem.at[i])
        for i, (source, target) in enumerate(
            [(pair, x), (mask, mk), (w_project, wp), (w_gate, wg), (w_output, wo)]
        )
    ]
    for d in range(8):
        for ty, tz in turned:
            signal(ahead(g, d), ty, tz)
    for d in range(1, 8):
        signal(g, y, ahead(z, d))
        signal(g, ahead(y, d), z)
        signal(ahead(g, d), y, z)
    for load in loads:
        load.start()

    def remote(u, n, source, target, who):
        return pltpu.make_async_remote_copy(
            src_ref=source, dst_ref=target, send_sem=s_sem.at[u, n], recv_sem=r_sem.at[u, n],
            device_id=device(*who), device_id_type=MESH,
        )

    def stay_refs(u):
        return (send_l, a_buf) if u == 0 else (send_r, b_buf)

    def cross_refs(u):
        return (send_r, b_buf) if u == 0 else (send_l, a_buf)

    def share_copy(u, e, sending):
        send, buf = stay_refs(u)
        to = partner(g, e)
        return remote(u, e, send.at[u, to], buf.at[u, 0, g if sending else to], (to, y, z))

    def turn_copy(u, e, sending):
        send, buf = cross_refs(u)
        to = partner(g, e)
        return remote(u, 8 + e, send.at[u, to], buf.at[u, 0, g if sending else to], (to, *turned[u]))

    def z_copy(u, d, piece):
        return remote(u, 16 + d, a_buf.at[u, 0, piece], a_buf.at[u, 8 - d, piece], (g, y, ahead(z, d)))

    def y_copy(u, d, piece):
        return remote(u, 24 + d, b_buf.at[u, 0, piece], b_buf.at[u, 8 - d, piece], (g, ahead(y, d), z))

    def block_wait(u, first, buf, slot):
        remote(u, first + lax.rem(8 - slot, 8), buf.at[u, 0], buf.at[u, slot], (g, y, z)).wait_recv()

    def back_copy(u, e, sending):
        to = partner(g, e)
        return remote(u, 32 + e, t_send.at[u, to], t_buf.at[u, g if sending else to], (to, y, z))

    FAR_FIRST = (4, 3, 5, 2, 6, 1, 7)
    NEAR_FIRST = (0, 2, 6, 4, 1, 3, 7, 5)

    def pack(u, send, operand):
        pieces = swap_blocks([operand[k] for k in range(8)])
        for p in range(8):
            send[u, p] = pieces[p].astype(BF16)

    def send_cross(u):
        for e in reversed(NEAR_FIRST):
            turn_copy(u, e, True).start()

    def send_stay(u):
        for e in reversed(NEAR_FIRST[1:]):
            share_copy(u, e, True).start()
        send, buf = stay_refs(u)
        buf[u, 0, g] = send[u, g]

    def exchange(u):
        copy = z_copy if u == 0 else y_copy
        for e in NEAR_FIRST:
            if e:
                share_copy(u, e, False).wait_recv()
            for d in FAR_FIRST:
                copy(u, d, partner(g, e)).start()
        copy = y_copy if u == 0 else z_copy
        for e in NEAR_FIRST:
            turn_copy(u, e, False).wait_recv()
            for d in FAR_FIRST:
                copy(u, d, partner(g, e)).start()
        for d in range(1, 8):
            block_wait(u, 16 if u == 0 else 24, stay_refs(u)[1], d)

    def widen(u, source, target):
        for p in range(8):
            x_hi, x_lo, core = p // 4, (p // 2) % 2, p % 2
            piece = source[p].astype(F32)
            if u == 0:
                first = (x_hi * 2 + core) * 8
                target[x_lo * 2, first : first + 8] = piece[:8]
                target[x_lo * 2 + 1, first : first + 8] = piece[8:]
            else:
                target[x_hi * 2 + core, x_lo * 16 : x_lo * 16 + 16] = piece

    def multiply(u):
        def block(t, _):
            odd = lax.rem(t, 2)
            cross = odd * ((t + 1) // 2) + (1 - odd) * lax.rem(8 - t // 2, 8)
            stay = lax.rem(HALF + 16 - cross + (z - y if u == 0 else y - z), 8)

            @pl.when(t > 0)
            def _():
                block_wait(u, 24 if u == 0 else 16, cross_refs(u)[1], cross)

            a_slot, b_slot = (stay, cross) if u == 0 else (cross, stay)
            widen(u, a_buf.at[u, a_slot], a_f)
            widen(u, b_buf.at[u, b_slot], b_f)

            def rows(c, _):
                total = [acc[c * 8 + i] for i in range(8)]
                for k in range(4):
                    b = b_f[k]
                    for i in range(8):
                        total[i] = total[i] + a_f[k, pl.ds(c * 8 + i, 1), :] * b
                for i in range(8):
                    acc[c * 8 + i] = total[i]
                return 0

            lax.fori_loop(0, 4, rows, 0)
            return 0

        lax.fori_loop(0, 8, block, 0)

    def give_back(u):
        for e in reversed(NEAR_FIRST):
            to = partner(g, e)
            row0, col0 = (to // 4 * 2 + to % 2) * 8, pl.multiple_of((to // 2) % 2 * 16, 16)
            t_send[u, to] = fold_blocks([acc[row0 + i, pl.ds(col0, 16), :] for i in range(8)])
            if e:
                back_copy(u, e, True).start()
        t_buf[u, g] = t_send[u, g]

    def output_gate(u):
        normed = norm_last(x[...]).astype(BF16)
        gate[...] = jax.nn.sigmoid(jnp.dot(normed, wg[u], preferred_element_type=F32))
        acc[...] = jnp.zeros_like(acc)

    def finish(u):
        for e in range(1, 8):
            back_copy(u, e, False).wait_recv()
        tri = jnp.concatenate(swap_blocks([t_buf[u, p] for p in range(8)]), axis=0)
        tnorm = norm_last(tri).astype(BF16)
        result = jnp.dot(tnorm, wo[u], preferred_element_type=F32)
        return x[...] + gate[...] * result

    def operand(normed, weight, w_proj):
        proj = jnp.dot(normed, w_proj, preferred_element_type=F32)
        return weight * jax.nn.sigmoid(proj[:, :128]) * proj[:, 128:]

    loads[0].wait()
    columns = [x[pl.ds(k, 8, stride=16), :] for k in range(16)]
    normed = norm_last(jnp.concatenate(columns, axis=0)).astype(BF16)
    loads[1].wait()
    mask_f = mk[...].astype(F32)
    weight = jnp.concatenate([jnp.broadcast_to(mask_f[:, k : k + 1], (8, 128)) for k in range(16)], axis=0)
    loads[2].wait()

    def by_steps(v):
        return jnp.swapaxes(v.reshape(2, 8, 8, 128), 0, 1).reshape(8, 16, 128)

    pack(0, send_r, by_steps(operand(normed, weight, wp[0, :, 256:])))
    pack(0, send_l, by_steps(operand(normed, weight, wp[0, :, :256])))
    pl.semaphore_wait(bar, 16 + 21)
    send_cross(0)
    send_stay(0)
    loads[3].wait()
    loads[4].wait()
    output_gate(0)
    r = lax.broadcasted_iota(jnp.int32, (128, 16), 0)
    c = lax.broadcasted_iota(jnp.int32, (128, 16), 1)
    spread = jnp.concatenate([jnp.broadcast_to(mask_f[i : i + 1, :], (16, 16)) for i in range(8)], axis=0)
    picked = jnp.where(r % 16 == c, spread, 0.0)
    mask_rows[...] = jnp.broadcast_to(jnp.sum(picked, axis=1, keepdims=True), (128, 128))
    exchange(0)
    multiply(0)
    give_back(0)
    x[...] = finish(0)

    normed = norm_last(x[...]).astype(BF16)
    pack(1, send_l, operand(normed, mask_rows[...], wp[1, :, :256]).reshape(8, 16, 128))
    send_cross(1)
    pack(1, send_r, operand(normed, mask_rows[...], wp[1, :, 256:]).reshape(8, 16, 128))
    send_stay(1)
    output_gate(1)
    exchange(1)
    multiply(1)
    give_back(1)
    out[...] = finish(1)

    for u in range(2):
        for e in range(8):
            turn_copy(u, e, True).wait_send()
            if e:
                share_copy(u, e, True).wait_send()
                back_copy(u, e, True).wait_send()
        for d in range(1, 8):
            for n, buf in ((16, a_buf), (24, b_buf)):
                remote(u, n + d, buf.at[u, 0], buf.at[u, 0], (g, y, z)).wait_send()


def per_device(pair, pair_mask, w_project, w_gate, w_output):
    hbm = pl.BlockSpec(memory_space=pltpu.HBM)
    updated = pl.pallas_call(
        kernel,
        name="triangle",
        out_shape=jax.ShapeDtypeStruct((128, 128), F32),
        in_specs=[hbm] * 5,
        out_specs=pl.BlockSpec(memory_space=pltpu.VMEM),
        scratch_shapes=[
            pltpu.VMEM((128, 128), F32),
            pltpu.VMEM((8, 16), jnp.int32),
            pltpu.VMEM((2, 128, 512), BF16),
            pltpu.VMEM((2, 128, 128), BF16),
            pltpu.VMEM((2, 128, 128), BF16),
            pltpu.VMEM((128, 128), F32),
            pltpu.VMEM((128, 128), F32),
            pltpu.VMEM((2, 8, 16, 128), BF16),
            pltpu.VMEM((2, 8, 16, 128), BF16),
            pltpu.VMEM((2, 8, 8, 16, 128), BF16),
            pltpu.VMEM((2, 8, 8, 16, 128), BF16),
            pltpu.VMEM((4, 32, 128), F32),
            pltpu.VMEM((4, 32, 128), F32),
            pltpu.VMEM((32, 32, 128), F32),
            pltpu.VMEM((2, 8, 16, 128), F32),
            pltpu.VMEM((2, 8, 16, 128), F32),
            pltpu.SemaphoreType.DMA((5,)),
            pltpu.SemaphoreType.DMA((2, 40)),
            pltpu.SemaphoreType.DMA((2, 40)),
        ],
        compiler_params=pltpu.CompilerParams(
            collective_id=0, has_side_effects=True, vmem_limit_bytes=32 * 1024 * 1024
        ),
    )(*(pltpu.with_memory_space_constraint(v, pltpu.HBM) for v in (pair.reshape(128, 128), pair_mask, w_project, w_gate, w_output)))
    return updated.reshape(pair.shape)


def solution(mesh):
    in_specs = (P("row", "col", None), P("row", "col"), P(), P(), P())
    return jax.shard_map(
        per_device, mesh=mesh, in_specs=in_specs, out_specs=P("row", "col", None), check_vma=False
    )
```

time: 62.8 us -> 55.5 us (0.88)
  local copies, waits for them, and re-layouts: 4.78 us -> 0.63 us
  Pallas kernels: 57.7 us -> 54.8 us
    unnamed x11 -> x1, local copies, waits for them, and re-layouts: 4.78 us -> 0.63 us
    pallas_call x1, Pallas kernels: 57.7 us -> 54.8 us  [per_device(): pl.pallas_call(kernel, name='triangle', out_shape=jax.ShapeDtypeStruct((1...]
where the time goes in v2:
time: 55.5 us; the launch traced here: 55.4 us
  Pallas kernels  54.8 us (99%)
  local copies, waits for them, and re-layouts  0.63 us (1%)
    pallas_call x1, Pallas kernels, per_device(): pl.pallas_call(kernel, name='triangle', out_shape=jax.ShapeDtypeStruct((1...  54.8 us

profile of v2, /device:TPU:1, one launch (start us, length us, event | category | flops | bytes accessed | tf_op | source)
XLA Modules:
  0.0 55.4 jit_solution(9320785620483472686)
XLA Ops:
  0.0 54.8 %triangle.1 = f32[128,128]{1,0:T(8,128)S(1)} custom-call(f32[128,128]{1,0:T(8,128)} %bitcast.3, s32[8,16]{1,0:T(8,128)} %mask.1, bf16[2,128,512]{2,1,0:T(8,128)(2,1)} %w_project.1, bf16[2,128,128]{2,1,0:T(8,128)(2,1)} %w_gate.1, bf16[2,128,128]{2,1,0:T(8,128)(2,1)} %w_output.1), custom_call_target="tpu_custom_call" | custom-call | tf_op jit(solution)/shard_map/triangle/pallas_call | solution.py:274
  54.8 0.6 %copy.7 = f32[8,16,128]{2,1,0:T(8,128)} copy(f32[8,16,128]{2,1,0:T(8,128)S(1)} %bitcast.2) | data formatting | bytes 131072

commit v3 on v2

v3 whole, which is shorter than its diff:
```python
import jax
import jax.numpy as jnp
from jax import lax
from jax.experimental import pallas as pl
from jax.experimental.pallas import tpu as pltpu
from jax.sharding import PartitionSpec as P

MESH = pl.DeviceIdType.MESH
F32, BF16 = jnp.float32, jnp.bfloat16
GROUP, RING, SHARE = 4, 8, 32
HALF = RING // 2


def coordinates():
    row, col = lax.axis_index("row"), lax.axis_index("col")
    return (row // 2) % 2 * 2 + col % 2, row % 2, row // 4, col // 2


def device(x, core, y, z):
    return ((y * 2 + x // 2) * 2 + core, z * 2 + x % 2)


def ahead(index, by):
    return lax.rem(index + by, RING)


def partner(x, e):
    return (x // 2 + e // 2) % 2 * 2 + (x + e) % 2


def barrel(parts):
    block = lax.broadcasted_iota(jnp.int32, parts[0].shape, 1) // SHARE
    for bit in (1, 2):
        odd = (block // bit) % 2 == 1
        parts = [jnp.where(odd, parts[(m + bit) % GROUP], parts[m]) for m in range(GROUP)]
    return parts


def rolled(parts):
    return [parts[0]] + [pltpu.roll(parts[m], SHARE * m, 1) for m in range(1, GROUP)]


def swap_blocks(parts):
    out = barrel(rolled(barrel(parts)))
    return [out[-g % GROUP] for g in range(GROUP)]


def fold_blocks(parts):
    turned = rolled(barrel(parts))
    return (turned[0] + turned[1]) + (turned[2] + turned[3])


def norm_last(values):
    center = values - jnp.mean(values, axis=-1, keepdims=True)
    spread = jnp.mean(center * center, axis=-1, keepdims=True)
    return center * lax.rsqrt(spread + 1e-05)


FAR_FIRST = (4, 3, 5, 2, 6, 1, 7)
NEAR_FIRST = (0, 1, 3, 2)
STAY, CROSS, ALONG_Z, ALONG_Y, BACK, CHIP = 0, 4, 8, 16, 24, 32
MATES = ((2, 1), (3, 1), (1, 1), (2, 0), (3, 0), (1, 0), (0, 1))


def kernel(
    pair, mask, w_project, w_gate, w_output, out,
    state, mk, wp, wg, wo, mask_rows, gate, send_l, send_r, a_buf, b_buf, a_far, wide_stay0, wide_cross0, wide_stay1,
    wide_cross1, acc0, acc1, t_send0, t_send1, t_buf0, t_buf1, in_sem, s_sem, r_sem,
):
    x, core, y, z = coordinates()
    other = 1 - core
    bar = pltpu.get_barrier_semaphore()
    turned = [(ahead(2 * y + HALF + 8, 8 - z), y), (z, ahead(2 * z + HALF + 8, 8 - y))]

    def signal(*who):
        pl.semaphore_signal(bar, inc=1, device_id=device(*who), device_id_type=MESH)

    for e in range(GROUP):
        for ty, tz in turned:
            signal(partner(x, e), core, ty, tz)
    for d in range(1, RING):
        signal(x, core, y, ahead(z, d))
        signal(x, core, ahead(y, d), z)
    for e, c in MATES:
        signal(partner(x, e), (core + c) % 2, y, z)
    loads = [
        pltpu.make_async_copy(source, target, in_sem.at[i])
        for i, (source, target) in enumerate(
            [(pair, state), (mask, mk), (w_project, wp), (w_gate, wg), (w_output, wo)]
        )
    ]
    for load in loads:
        load.start()

    def remote(u, n, source, target, who):
        return pltpu.make_async_remote_copy(
            src_ref=source, dst_ref=target, send_sem=s_sem.at[u, n], recv_sem=r_sem.at[u, n],
            device_id=device(*who), device_id_type=MESH,
        )

    def stay_refs(u):
        return (send_l, a_buf) if u == 0 else (send_r, b_buf)

    def cross_refs(u):
        return (send_r, b_buf) if u == 0 else (send_l, a_buf)

    def share_copy(u, e, sending):
        send, buf = stay_refs(u)
        to = partner(x, e)
        return remote(u, STAY + e, send.at[u, to], buf.at[u, 0, x if sending else to], (to, core, y, z))

    def turn_copy(u, e, sending):
        send, buf = cross_refs(u)
        to = partner(x, e)
        return remote(u, CROSS + e, send.at[u, to], buf.at[u, 0, x if sending else to], (to, core, *turned[u]))

    def z_copy(u, d, piece):
        return remote(
            u, ALONG_Z + d, a_buf.at[u, 0, piece], a_buf.at[u, 8 - d, piece], (x, core, y, ahead(z, d))
        )

    def y_copy(u, d, piece):
        return remote(
            u, ALONG_Y + d, b_buf.at[u, 0, piece], b_buf.at[u, 8 - d, piece], (x, core, ahead(y, d), z)
        )

    def block_wait(u, first, buf, slot):
        remote(u, first + lax.rem(8 - slot, 8), buf.at[u, 0], buf.at[u, slot], (x, core, y, z)).wait_recv()

    def back_copy(u, e, c, sending):
        send, buf = (t_send0, t_buf0) if u == 0 else (t_send1, t_buf1)
        to, to_core = partner(x, e), (core + c) % 2
        slot = (x, core) if sending else (to, to_core)
        return remote(u, BACK + 2 * e + c, send.at[to, to_core], buf.at[slot], (to, to_core, y, z))

    def block_to_other(slot):
        return remote(0, CHIP + slot, a_buf.at[0, slot], a_far.at[slot], (x, other, y, z))

    def pack(u, send, operand):
        steps = operand.reshape(4, 4, 8, 128) if u == 0 else operand.reshape(2, 4, 16, 128)
        pieces = swap_blocks([steps[:, k].reshape(32, 128) for k in range(GROUP)])
        for p in range(GROUP):
            send[u, p] = pieces[p].astype(BF16)

    def send_cross(u):
        for e in reversed(NEAR_FIRST):
            turn_copy(u, e, True).start()

    def send_stay(u):
        for e in reversed(NEAR_FIRST[1:]):
            share_copy(u, e, True).start()
        send, buf = stay_refs(u)
        buf[u, 0, x] = send[u, x]

    def widen(u, source, target):
        for p in range(GROUP):
            x_hi, x_lo = p // 2, p % 2
            piece = source[p].astype(F32)
            if u == 0:
                target[x_lo * 4 : x_lo * 4 + 4, x_hi * 8 : x_hi * 8 + 8] = piece.reshape(4, 8, 128)
            else:
                target[x_hi * 2 : x_hi * 2 + 2, x_lo * 16 : x_lo * 16 + 16] = piece.reshape(2, 16, 128)

    def exchange(u):
        copy = z_copy if u == 0 else y_copy
        for e in NEAR_FIRST:
            if e:
                share_copy(u, e, False).wait_recv()
            for d in FAR_FIRST:
                copy(u, d, partner(x, e)).start()
        copy = y_copy if u == 0 else z_copy
        for e in NEAR_FIRST:
            turn_copy(u, e, False).wait_recv()
            for d in FAR_FIRST:
                copy(u, d, partner(x, e)).start()
        if u == 0:
            def arrive(slot, _):
                @pl.when(slot > 0)
                def _():
                    block_wait(0, ALONG_Z, a_buf, slot)

                block_to_other(slot).start()
                widen(0, a_buf.at[0, slot], wide_stay0.at[0, slot])
                return 0

            def arrive_other(slot, _):
                block_to_other(slot).wait_recv()
                widen(0, a_far.at[slot], wide_stay0.at[1, slot])
                return 0

            lax.fori_loop(0, 8, arrive, 0)
            lax.fori_loop(0, 8, arrive_other, 0)
        else:
            def arrive(slot, _):
                @pl.when(slot > 0)
                def _():
                    block_wait(1, ALONG_Y, b_buf, slot)

                widen(1, b_buf.at[1, slot], wide_stay1.at[slot])
                return 0

            lax.fori_loop(0, 8, arrive, 0)

    def nearest(t):
        odd = lax.rem(t, 2)
        return odd * ((t + 1) // 2) + (1 - odd) * lax.rem(8 - t // 2, 8)

    def stay_slot(u, cross):
        return lax.rem(HALF + 16 - cross + (z - y if u == 0 else y - z), 8)

    def multiply_first():
        def block(t, _):
            slot = nearest(t)

            @pl.when(t > 0)
            def _():
                block_wait(0, ALONG_Y, b_buf, slot)

            widen(0, b_buf.at[0, slot], wide_cross0)
            stay = stay_slot(0, slot)

            def rows(half, _):
                total = [acc0[half, i] for i in range(16)]
                for k in range(8):
                    b = wide_cross0[k]
                    for i in range(16):
                        total[i] = total[i] + wide_stay0[half, stay, k, pl.ds(i, 1), :] * b
                for i in range(16):
                    acc0[half, i] = total[i]
                return 0

            lax.fori_loop(0, 2, rows, 0)
            return 0

        lax.fori_loop(0, 8, block, 0)

    def multiply_second():
        def block(t, _):
            slot = nearest(t)

            @pl.when(t > 0)
            def _():
                block_wait(1, ALONG_Z, a_buf, slot)

            widen(1, a_buf.at[1, slot], wide_cross1)
            stay = stay_slot(1, slot)

            def rows(c, _):
                total = [acc1[c * 8 + i] for i in range(8)]
                for k in range(4):
                    b = wide_stay1[stay, k]
                    for i in range(8):
                        total[i] = total[i] + wide_cross1[k, pl.ds(c * 8 + i, 1), :] * b
                for i in range(8):
                    acc1[c * 8 + i] = total[i]
                return 0

            lax.fori_loop(0, 4, rows, 0)
            return 0

        lax.fori_loop(0, 8, block, 0)

    def give_back(u):
        def piece(to, c):
            if u == 0:
                columns = pl.ds(pl.multiple_of(to % 2 * 8, 8), 8)
                rows = [acc0[c, to // 2 * 8 + i, columns, :] for i in range(8)]
            else:
                columns = pl.ds(pl.multiple_of(to % 2 * 16, 16), 16)
                first = (to // 2 * 2 + (core + c) % 2) * 8
                rows = [acc1[first + i, columns, :] for i in range(8)]
            return jnp.concatenate([fold_blocks(rows[:GROUP]), fold_blocks(rows[GROUP:])], axis=0)

        send, buf = (t_send0, t_buf0) if u == 0 else (t_send1, t_buf1)
        for e, c in MATES:
            to = partner(x, e)
            send[to, (core + c) % 2] = piece(to, c)
            back_copy(u, e, c, True).start()
        buf[x, core] = piece(x, 0)

    def output_gate(u):
        normed = norm_last(state[...]).astype(BF16)
        gate[...] = jax.nn.sigmoid(jnp.dot(normed, wg[u], preferred_element_type=F32))
        acc = acc0 if u == 0 else acc1
        acc[...] = jnp.zeros_like(acc)

    def finish(u):
        for e, c in MATES:
            back_copy(u, e, c, False).wait_recv()
        if u == 0:
            parts = [
                jnp.stack([t_buf0[p, c].reshape(2, 8, 128) for c in range(2)], axis=1).reshape(32, 128)
                for p in range(GROUP)
            ]
        else:
            parts = [t_buf1[p, 0] + t_buf1[p, 1] for p in range(GROUP)]
        parts = swap_blocks(parts)
        tri = jnp.stack([part.reshape(2, 16, 128) for part in parts], axis=1).reshape(128, 128)
        tnorm = norm_last(tri).astype(BF16)
        result = jnp.dot(tnorm, wo[u], preferred_element_type=F32)
        return state[...] + gate[...] * result

    def operand(normed, weight, w_proj):
        proj = jnp.dot(normed, w_proj, preferred_element_type=F32)
        return weight * jax.nn.sigmoid(proj[:, :128]) * proj[:, 128:]

    loads[0].wait()
    columns = [state[pl.ds(k, 8, stride=16), :] for k in range(16)]
    normed = norm_last(jnp.concatenate(columns, axis=0)).astype(BF16)
    loads[1].wait()
    mask_f = mk[...].astype(F32)
    weight = jnp.concatenate([jnp.broadcast_to(mask_f[:, k : k + 1], (8, 128)) for k in range(16)], axis=0)
    loads[2].wait()
    pack(0, send_r, operand(normed, weight, wp[0, :, 256:]))
    pack(0, send_l, operand(normed, weight, wp[0, :, :256]))
    pl.semaphore_wait(bar, 2 * GROUP + 2 * (RING - 1) + len(MATES))
    send_cross(0)
    send_stay(0)
    loads[3].wait()
    loads[4].wait()
    output_gate(0)
    r = lax.broadcasted_iota(jnp.int32, (128, 16), 0)
    c = lax.broadcasted_iota(jnp.int32, (128, 16), 1)
    spread = jnp.concatenate([jnp.broadcast_to(mask_f[i : i + 1, :], (16, 16)) for i in range(8)], axis=0)
    picked = jnp.where(r % 16 == c, spread, 0.0)
    mask_rows[...] = jnp.broadcast_to(jnp.sum(picked, axis=1, keepdims=True), (128, 128))
    exchange(0)
    multiply_first()
    give_back(0)
    state[...] = finish(0)

    normed = norm_last(state[...]).astype(BF16)
    pack(1, send_l, operand(normed, mask_rows[...], wp[1, :, :256]))
    send_cross(1)
    pack(1, send_r, operand(normed, mask_rows[...], wp[1, :, 256:]))
    send_stay(1)
    output_gate(1)
    exchange(1)
    multiply_second()
    give_back(1)
    out[...] = finish(1)

    for u in range(2):
        for e in range(GROUP):
            turn_copy(u, e, True).wait_send()
            if e:
                share_copy(u, e, True).wait_send()
        for e, c in MATES:
            back_copy(u, e, c, True).wait_send()
        for d in range(1, RING):
            for n, buf in ((ALONG_Z, a_buf), (ALONG_Y, b_buf)):
                remote(u, n + d, buf.at[u, 0], buf.at[u, 0], (x, core, y, z)).wait_send()
    for slot in range(RING):
        block_to_other(slot).wait_send()


def per_device(pair, pair_mask, w_project, w_gate, w_output):
    hbm = pl.BlockSpec(memory_space=pltpu.HBM)
    operands = (pair.reshape(128, 128), pair_mask, w_project, w_gate, w_output)
    updated = pl.pallas_call(
        kernel,
        name="triangle",
        out_shape=jax.ShapeDtypeStruct((128, 128), F32),
        in_specs=[hbm] * 5,
        out_specs=pl.BlockSpec(memory_space=pltpu.VMEM),
        scratch_shapes=[
            pltpu.VMEM((128, 128), F32),
            pltpu.VMEM((8, 16), jnp.int32),
            pltpu.VMEM((2, 128, 512), BF16),
            pltpu.VMEM((2, 128, 128), BF16),
            pltpu.VMEM((2, 128, 128), BF16),
            pltpu.VMEM((128, 128), F32),
            pltpu.VMEM((128, 128), F32),
            pltpu.VMEM((2, 4, 32, 128), BF16),
            pltpu.VMEM((2, 4, 32, 128), BF16),
            pltpu.VMEM((2, 8, 4, 32, 128), BF16),
            pltpu.VMEM((2, 8, 4, 32, 128), BF16),
            pltpu.VMEM((8, 4, 32, 128), BF16),
            pltpu.VMEM((2, 8, 8, 16, 128), F32),
            pltpu.VMEM((8, 16, 128), F32),
            pltpu.VMEM((8, 4, 32, 128), F32),
            pltpu.VMEM((4, 32, 128), F32),
            pltpu.VMEM((2, 16, 16, 128), F32),
            pltpu.VMEM((32, 32, 128), F32),
            pltpu.VMEM((4, 2, 16, 128), F32),
            pltpu.VMEM((4, 2, 32, 128), F32),
            pltpu.VMEM((4, 2, 16, 128), F32),
            pltpu.VMEM((4, 2, 32, 128), F32),
            pltpu.SemaphoreType.DMA((5,)),
            pltpu.SemaphoreType.DMA((2, 40)),
            pltpu.SemaphoreType.DMA((2, 40)),
        ],
        compiler_params=pltpu.CompilerParams(
            collective_id=0, has_side_effects=True, vmem_limit_bytes=32 * 1024 * 1024
        ),
    )(*(pltpu.with_memory_space_constraint(value, pltpu.HBM) for value in operands))
    return updated.reshape(pair.shape)


def solution(mesh):
    in_specs = (P("row", "col", None), P("row", "col"), P(), P(), P())
    return jax.shard_map(
        per_device, mesh=mesh, in_specs=in_specs, out_specs=P("row", "col", None), check_vma=False
    )
```

time: 55.5 us -> 54.5 us (0.982)
  Pallas kernels: 54.8 us -> 53.7 us
    pallas_call x1, Pallas kernels: 54.8 us -> 53.7 us  [per_device(): pl.pallas_call(kernel, name='triangle', out_shape=jax.ShapeDtypeStruct((1...]
where the time goes in v3:
time: 54.5 us; the launch traced here: 54.3 us
  Pallas kernels  53.7 us (99%)
  local copies, waits for them, and re-layouts  0.63 us (1%)
    pallas_call x1, Pallas kernels, per_device(): pl.pallas_call(kernel, name='triangle', out_shape=jax.ShapeDtypeStruct((1...  53.7 us

profile of v3, /device:TPU:1, one launch (start us, length us, event | category | flops | bytes accessed | tf_op | source)
XLA Modules:
  0.0 54.3 jit_solution(4125467995445960122)
XLA Ops:
  0.0 53.7 %triangle.1 = f32[128,128]{1,0:T(8,128)S(1)} custom-call(f32[128,128]{1,0:T(8,128)} %bitcast.3, s32[8,16]{1,0:T(8,128)} %mask.1, bf16[2,128,512]{2,1,0:T(8,128)(2,1)} %w_project.1, bf16[2,128,128]{2,1,0:T(8,128)(2,1)} %w_gate.1, bf16[2,128,128]{2,1,0:T(8,128)(2,1)} %w_output.1), custom_call_target="tpu_custom_call" | custom-call | tf_op jit(solution)/shard_map/triangle/pallas_call | solution.py:360
  53.7 0.6 %copy.7 = f32[8,16,128]{2,1,0:T(8,128)} copy(f32[8,16,128]{2,1,0:T(8,128)S(1)} %bitcast.2) | data formatting | bytes 131072

commit v4 on v3

--- a/solution.py
+++ b/solution.py
@@ -70,13 +70,14 @@
     x, core, y, z = coordinates()
     other = 1 - core
     bar = pltpu.get_barrier_semaphore()
-    turned = [(ahead(2 * y + HALF + 8, 8 - z), y), (z, ahead(2 * z + HALF + 8, 8 - y))]
+    turned = [(ahead(2 * y + HALF + 8, 8 - z), y), (z, ahead(y, HALF))]
+    sources = [(z, ahead(2 * z + HALF + 8, 8 - y)), (ahead(z, HALF), y)]
 
     def signal(*who):
         pl.semaphore_signal(bar, inc=1, device_id=device(*who), device_id_type=MESH)
 
     for e in range(GROUP):
-        for ty, tz in turned:
+        for ty, tz in sources:
             signal(partner(x, e), core, ty, tz)
     for d in range(1, RING):
         signal(x, core, y, ahead(z, d))
@@ -206,7 +207,9 @@
         return odd * ((t + 1) // 2) + (1 - odd) * lax.rem(8 - t // 2, 8)
 
     def stay_slot(u, cross):
-        return lax.rem(HALF + 16 - cross + (z - y if u == 0 else y - z), 8)
+        if u == 1:
+            return lax.rem(HALF + 8 + cross + z - y, 8)
+        return lax.rem(HALF + 16 - cross + z - y, 8)
 
     def multiply_first():
         def block(t, _):
@@ -303,6 +306,20 @@
     def operand(normed, weight, w_proj):
         proj = jnp.dot(normed, w_proj, preferred_element_type=F32)
         return weight * jax.nn.sigmoid(proj[:, :128]) * proj[:, 128:]
+
+    def sent(u):
+        for e in range(GROUP):
+            turn_copy(u, e, True).wait_send()
+            if e:
+                share_copy(u, e, True).wait_send()
+        for e, c in MATES:
+            back_copy(u, e, c, True).wait_send()
+        for d in range(1, RING):
+            for n, buf in ((ALONG_Z, a_buf), (ALONG_Y, b_buf)):
+                remote(u, n + d, buf.at[u, 0], buf.at[u, 0], (x, core, y, z)).wait_send()
+        if u == 0:
+            for slot in range(RING):
+                block_to_other(slot).wait_send()
 
     loads[0].wait()
     columns = [state[pl.ds(k, 8, stride=16), :] for k in range(16)]
@@ -335,23 +352,12 @@
     pack(1, send_r, operand(normed, mask_rows[...], wp[1, :, 256:]))
     send_stay(1)
     output_gate(1)
+    sent(0)
     exchange(1)
     multiply_second()
     give_back(1)
+    sent(1)
     out[...] = finish(1)
-
-    for u in range(2):
-        for e in range(GROUP):
-            turn_copy(u, e, True).wait_send()
-            if e:
-                share_copy(u, e, True).wait_send()
-        for e, c in MATES:
-            back_copy(u, e, c, True).wait_send()
-        for d in range(1, RING):
-            for n, buf in ((ALONG_Z, a_buf), (ALONG_Y, b_buf)):
-                remote(u, n + d, buf.at[u, 0], buf.at[u, 0], (x, core, y, z)).wait_send()
-    for slot in range(RING):
-        block_to_other(slot).wait_send()
 
 
 def per_device(pair, pair_mask, w_project, w_gate, w_output):

time: 54.5 us -> 54.4 us (level)
  no operation moved by 1% of the time
where the time goes in v4:
time: 54.4 us; the launch traced here: 54.3 us
  Pallas kernels  53.6 us (99%)
  local copies, waits for them, and re-layouts  0.63 us (1%)
    pallas_call x1, Pallas kernels, per_device(): pl.pallas_call(kernel, name='triangle', out_shape=jax.ShapeDtypeStruct((1...  53.6 us

profile of v4, /device:TPU:1, one launch (start us, length us, event | category | flops | bytes accessed | tf_op | source)
XLA Modules:
  0.0 54.3 jit_solution(15312960765619431792)
XLA Ops:
  0.0 53.6 %triangle.1 = f32[128,128]{1,0:T(8,128)S(1)} custom-call(f32[128,128]{1,0:T(8,128)} %bitcast.3, s32[8,16]{1,0:T(8,128)} %mask.1, bf16[2,128,512]{2,1,0:T(8,128)(2,1)} %w_project.1, bf16[2,128,128]{2,1,0:T(8,128)(2,1)} %w_gate.1, bf16[2,128,128]{2,1,0:T(8,128)(2,1)} %w_output.1), custom_call_target="tpu_custom_call" | custom-call | tf_op jit(solution)/shard_map/triangle/pallas_call | solution.py:366
  53.6 0.6 %copy.7 = f32[8,16,128]{2,1,0:T(8,128)} copy(f32[8,16,128]{2,1,0:T(8,128)S(1)} %bitcast.2) | data formatting | bytes 131072

commit v5 on v4

--- a/solution.py
+++ b/solution.py
@@ -162,13 +162,17 @@
             else:
                 target[x_hi * 2 : x_hi * 2 + 2, x_lo * 16 : x_lo * 16 + 16] = piece.reshape(2, 16, 128)
 
+    def both(e):
+        return pl.ds(partner(x, e) // 2 * 2, 2)
+
     def exchange(u):
         copy = z_copy if u == 0 else y_copy
-        for e in NEAR_FIRST:
-            if e:
-                share_copy(u, e, False).wait_recv()
+        for pair in (NEAR_FIRST[:2], NEAR_FIRST[2:]):
+            for e in pair:
+                if e:
+                    share_copy(u, e, False).wait_recv()
             for d in FAR_FIRST:
-                copy(u, d, partner(x, e)).start()
+                copy(u, d, both(pair[0])).start()
         copy = y_copy if u == 0 else z_copy
         for e in NEAR_FIRST:
             turn_copy(u, e, False).wait_recv()

time: 54.4 us -> 54.6 us (level)
  no operation moved by 1% of the time
where the time goes in v5:
time: 54.6 us; the launch traced here: 54.4 us
  Pallas kernels  53.8 us (99%)
  local copies, waits for them, and re-layouts  0.63 us (1%)
    pallas_call x1, Pallas kernels, per_device(): pl.pallas_call(kernel, name='triangle', out_shape=jax.ShapeDtypeStruct((1...  53.8 us

profile of v5, /device:TPU:1, one launch (start us, length us, event | category | flops | bytes accessed | tf_op | source)
XLA Modules:
  0.0 54.4 jit_solution(13405506581771400654)
XLA Ops:
  0.0 53.8 %triangle.1 = f32[128,128]{1,0:T(8,128)S(1)} custom-call(f32[128,128]{1,0:T(8,128)} %bitcast.3, s32[8,16]{1,0:T(8,128)} %mask.1, bf16[2,128,512]{2,1,0:T(8,128)(2,1)} %w_project.1, bf16[2,128,128]{2,1,0:T(8,128)(2,1)} %w_gate.1, bf16[2,128,128]{2,1,0:T(8,128)(2,1)} %w_output.1), custom_call_target="tpu_custom_call" | custom-call | tf_op jit(solution)/shard_map/triangle/pallas_call | solution.py:370
  53.8 0.6 %copy.7 = f32[8,16,128]{2,1,0:T(8,128)} copy(f32[8,16,128]{2,1,0:T(8,128)S(1)} %bitcast.2) | data formatting | bytes 131072
